TPU v7x, 32 devices: a whole 2x2x4 slice. The times are simulated.
32 devices in a mesh: frames: 16 (over z, y, x), rows: 2 (over core).
Axes of the slice: x: 2, y: 2, z: 4, core: 2. Of those that a mesh axis runs over, the one named last changes fastest.
Arguments:
- video: bfloat16 [128, 8, 16, 384], P('frames', 'rows'), may hold values from -6 to 6
- counts: int32 [16], replicated, may hold values from 1 to 8, as said below
- down_weight: bfloat16 [9, 384, 384], replicated, may hold values from -0.109375 to 0.109375
- spatial_conv_bias: float32 [384], replicated, may hold values from -1.5 to 1.5
- time_weight: bfloat16 [3, 384, 384], replicated, may hold values from -0.1875 to 0.1875
- time_bias: float32 [384], replicated, may hold values from -1.5 to 1.5
- norm1_gain: float32 [384], replicated, may hold values from 0.1 to 1.9
- conv1_weight: bfloat16 [27, 384, 384], P(None, 'rows'), may hold values from -0.0625 to 0.0625
- conv1_bias: float32 [384], P('rows'), may hold values from -1.5 to 1.5
- norm2_gain: float32 [384], replicated, may hold values from 0.1 to 1.9
- conv2_weight: bfloat16 [27, 384, 384], P(None, 'rows'), may hold values from -0.0625 to 0.0625
- conv2_bias: float32 [384], P('rows'), may hold values from -1.5 to 1.5
Outputs:
- latents: bfloat16 [64, 4, 8, 384], P('frames', 'rows')
Inputs may be any that keep to these rules, and one draw needn't show every extreme that they name: `counts`: entry 0 is 1; every other entry is even and at least 4; some entry equals 8.
All inputs are finite; a program needn't handle non-finite values.
Results may differ from a plain program's by a relative error of at most 0.0065.
Values may be sent and summed in bfloat16 or wider, within the bound.
A program may use at most 64 MiB of HBM per device.

v0:
```python
import jax
import jax.numpy as jnp
from jax import lax
from jax.sharding import PartitionSpec as P

epsilon = 1e-06


def shifted(value, axis, steps):
    count = lax.axis_size(axis)
    initial, last = (max(0, -steps), min(count, count - steps))
    return lax.ppermute(value, axis, [(source, source + steps) for source in range(initial, last)])


def rms_scale(values, gain_vec):
    mean_sq = jnp.mean(values * values, axis=-1, keepdims=True)
    return values * lax.rsqrt(mean_sq + epsilon) * gain_vec


def conv_taps(padded, weight, frames_out, rows_out, cols_out):
    running = None
    for tap_t in range(3):
        for tap_r in range(3):
            for tap_c in range(3):
                window = padded[
                    tap_t : tap_t + frames_out, tap_r : tap_r + rows_out, tap_c : tap_c + cols_out
                ]
                flat_rows = window.reshape(-1, window.shape[-1])
                partial_term = lax.dot_general(
                    flat_rows,
                    weight[tap_t * 9 + tap_r * 3 + tap_c],
                    (((1,), (1,)), ((), ())),
                    preferred_element_type=jnp.float32,
                )
                running = partial_term if running is None else running + partial_term
    return running.reshape(frames_out, rows_out, cols_out, weight.shape[1])


def pad_space(values):
    return jnp.pad(values, ((0, 0), (1, 1), (1, 1), (0, 0)))


def last_two(values, live_count):
    with_front = jnp.concatenate([jnp.zeros((2,) + values.shape[1:], values.dtype), values], axis=0)
    return lax.dynamic_slice_in_dim(with_front, live_count, 2, 0)


def per_device(
    video,
    counts,
    down_weight,
    spatial_conv_bias,
    time_weight,
    time_bias,
    norm1_gain,
    conv1_weight,
    conv1_bias,
    norm2_gain,
    conv2_weight,
    conv2_bias,
):
    frame_slots, in_rows, in_cols, channels = video.shape
    out_slots = frame_slots // 2
    out_rows = in_rows // 2
    out_cols = in_cols // 2
    position = lax.axis_index("frames")
    shard_total = counts.shape[0]
    own_count = jnp.sum(jnp.where(jnp.arange(shard_total, dtype=jnp.int32) == position, counts, 0))
    is_first = position == 0
    live_count = jnp.where(is_first, 1, own_count // 2)
    lower_row = shifted(video[:, :1], "rows", -1)
    extended = jnp.concatenate([video, lower_row], axis=1)
    extended = jnp.pad(extended, ((0, 0), (0, 0), (0, 1), (0, 0)))
    spatial_result = None
    for tap_r in range(3):
        for tap_c in range(3):
            window = extended[:, tap_r : tap_r + 2 * out_rows : 2, tap_c : tap_c + 2 * out_cols : 2]
            partial_term = jnp.dot(
                window.reshape(-1, channels),
                down_weight[tap_r * 3 + tap_c],
                preferred_element_type=jnp.float32,
            )
            spatial_result = (
                partial_term if spatial_result is None else spatial_result + partial_term
            )
    halved_frames = (
        (spatial_result + spatial_conv_bias)
        .astype(jnp.bfloat16)
        .reshape(frame_slots, out_rows, out_cols, channels)
    )
    last_frame = lax.dynamic_slice_in_dim(halved_frames, own_count - 1, 1, 0)
    before = shifted(last_frame, "frames", 1)
    timeline = jnp.concatenate([before, halved_frames], axis=0)
    merged = None
    for tap_t in range(3):
        window = timeline[tap_t : tap_t + 2 * out_slots : 2]
        partial_term = jnp.dot(
            window.reshape(-1, channels), time_weight[tap_t], preferred_element_type=jnp.float32
        )
        merged = partial_term if merged is None else merged + partial_term
    merged = (merged + time_bias).reshape(out_slots, out_rows, out_cols, channels)
    slot_numbers = jnp.arange(out_slots, dtype=jnp.int32).reshape(-1, 1, 1, 1)
    keep_first = jnp.logical_and(is_first, slot_numbers == 0)
    latent_in = jnp.where(keep_first, halved_frames[:out_slots].astype(jnp.float32), merged).astype(
        jnp.bfloat16
    )
    act_one = jax.nn.silu(rms_scale(latent_in.astype(jnp.float32), norm1_gain)).astype(jnp.bfloat16)
    prior_one = shifted(last_two(act_one, live_count), "frames", 1)
    whole_one = lax.all_gather(
        jnp.concatenate([prior_one, act_one], axis=0), "rows", axis=1, tiled=True
    )
    all_rows = whole_one.shape[1]
    part_one = (
        conv_taps(pad_space(whole_one), conv1_weight, out_slots, all_rows, out_cols) + conv1_bias
    ).astype(jnp.bfloat16)
    hidden_one = lax.all_to_all(part_one, "rows", split_axis=1, concat_axis=3, tiled=True)
    act_two = jax.nn.silu(rms_scale(hidden_one.astype(jnp.float32), norm2_gain)).astype(
        jnp.bfloat16
    )
    prior_two = shifted(last_two(act_two, live_count), "frames", 1)
    whole_two = lax.all_gather(
        jnp.concatenate([prior_two, act_two], axis=0), "rows", axis=1, tiled=True
    )
    part_two = (
        conv_taps(pad_space(whole_two), conv2_weight, out_slots, all_rows, out_cols) + conv2_bias
    ).astype(jnp.bfloat16)
    hidden_two = lax.all_to_all(part_two, "rows", split_axis=1, concat_axis=3, tiled=True)
    result = latent_in.astype(jnp.float32) + hidden_two.astype(jnp.float32)
    result = jnp.where(slot_numbers < live_count, result, 0.0)
    return result.astype(jnp.bfloat16)


def solution(mesh):
    in_specs = (
        P("frames", "rows", None, None),
        P(),
        P(),
        P(),
        P(),
        P(),
        P(),
        P(None, "rows", None),
        P("rows"),
        P(),
        P(None, "rows", None),
        P("rows"),
    )
    out_specs = P("frames", "rows", None, None)
    return jax.shard_map(
        per_device, mesh=mesh, in_specs=in_specs, out_specs=out_specs, check_vma=False
    )
```

profile of v0, /device:TPU:25, one launch (start us, length us, event | category | flops | bytes accessed | tf_op | source)
XLA Modules:
  0.0 108.1 jit_solution(14506700439245783793)
XLA Ops:
  0.0 1.1 slice.409
  1.1 2.6 %collective-permute-start = (bf16[8,1,16,384]{3,2,1,0:T(8,128)(2,1)S(1)}, bf16[8,1,16,384]{3,2,1,0:T(8,128)(2,1)S(1)}, u32[]{:S(2)}, u32[]{:S(2)}) collective-permute-start(bf16[8,1,16,384]{3,2,1,0:T(8,128)(2,1)S(1)} %slice.409), channel_id=1, source_target_pairs={{1,0},{3,2},{5,4},{7,6},{9,8},{11,10},{13,12},{15,14},{17,16},{19,... | collective-permute-start | bytes 294920 | tf_op jit(solution)/shard_map/ppermute | solution.py:12
  3.7 1.3 %fusion.153 = s32[]{:T(128)} fusion(s32[16]{0:T(128)} %param.13, s32[]{:T(128)S(6)} %axis_index.15), kind=kLoop, calls=%fused_computation.284 | loop fusion | flops 47 | bytes 72 | tf_op jit(solution)/shard_map/reduce_sum | solution.py:68
  9.0 1.1 fusion.5
  10.1 0.9 slice.424
  11.0 5.0 %slice.422 = bf16[8,2,8,384]{3,2,1,0:T(8,128)(2,1)} slice(bf16[8,5,17,384]{3,2,1,0:T(8,128)(2,1)S(1)} %fusion.5), slice={[0:8:1], [2:5:2], [0:16:2], [0:384:1]} | slice | bytes 196608 | tf_op jit(solution)/shard_map/slice | solution.py:77
  16.0 5.0 %slice.420 = bf16[8,2,8,384]{3,2,1,0:T(8,128)(2,1)} slice(bf16[8,5,17,384]{3,2,1,0:T(8,128)(2,1)S(1)} %fusion.5), slice={[0:8:1], [1:5:2], [2:17:2], [0:384:1]} | slice | bytes 196608 | tf_op jit(solution)/shard_map/slice | solution.py:77
  21.0 4.9 %slice.418 = bf16[8,2,8,384]{3,2,1,0:T(8,128)(2,1)} slice(bf16[8,5,17,384]{3,2,1,0:T(8,128)(2,1)S(1)} %fusion.5), slice={[0:8:1], [1:5:2], [1:17:2], [0:384:1]} | slice | bytes 196608 | tf_op jit(solution)/shard_map/slice | solution.py:77
  25.9 4.9 %slice.416 = bf16[8,2,8,384]{3,2,1,0:T(8,128)(2,1)} slice(bf16[8,5,17,384]{3,2,1,0:T(8,128)(2,1)S(1)} %fusion.5), slice={[0:8:1], [1:5:2], [0:16:2], [0:384:1]} | slice | bytes 196608 | tf_op jit(solution)/shard_map/slice | solution.py:77
  30.8 4.9 %slice.414 = bf16[8,2,8,384]{3,2,1,0:T(8,128)(2,1)} slice(bf16[8,5,17,384]{3,2,1,0:T(8,128)(2,1)S(1)} %fusion.5), slice={[0:8:1], [0:4:2], [2:17:2], [0:384:1]} | slice | bytes 196608 | tf_op jit(solution)/shard_map/slice | solution.py:77
  35.8 4.9 %slice.412 = bf16[8,2,8,384]{3,2,1,0:T(8,128)(2,1)} slice(bf16[8,5,17,384]{3,2,1,0:T(8,128)(2,1)S(1)} %fusion.5), slice={[0:8:1], [0:4:2], [1:17:2], [0:384:1]} | slice | bytes 196608 | tf_op jit(solution)/shard_map/slice | solution.py:77
  40.7 4.9 %slice.410 = bf16[8,2,8,384]{3,2,1,0:T(8,128)(2,1)} slice(bf16[8,5,17,384]{3,2,1,0:T(8,128)(2,1)S(1)} %fusion.5), slice={[0:8:1], [0:4:2], [0:16:2], [0:384:1]} | slice | bytes 196608 | tf_op jit(solution)/shard_map/slice | solution.py:77
  45.6 5.0 %slice.426 = bf16[8,2,8,384]{3,2,1,0:T(8,128)(2,1)} slice(bf16[8,5,17,384]{3,2,1,0:T(8,128)(2,1)S(1)} %fusion.5), slice={[0:8:1], [2:5:2], [2:17:2], [0:384:1]} | slice | bytes 196608 | tf_op jit(solution)/shard_map/slice | solution.py:77
  50.6 1.3 %fusion.18 = f32[128,384]{1,0:T(8,128)S(1)} fusion(bf16[128,384]{1,0:T(8,128)(2,1)} %bitcast.414, bf16[9,384,384]{2,1,0:T(8,128)(2,1)} %param.14), kind=kOutput, calls=%fused_computation.129 | convolution fusion | flops 37748736 | bytes 589824 | tf_op jit(solution)/shard_map/dot_general | solution.py:78
  51.9 1.1 %convolution_add_fusion.7 = f32[128,384]{1,0:T(8,128)S(1)} fusion(f32[128,384]{1,0:T(8,128)S(1)} %fusion.18, bf16[128,384]{1,0:T(8,128)(2,1)} %bitcast.413, bf16[9,384,384]{2,1,0:T(8,128)(2,1)S(1)} %copy-done.2), kind=kOutput, calls=%fused_computation.59 | convolution fusion | flops 37797888 | bytes 786432 | tf_op jit(solution)/shard_map/dot_general | solution.py:78
  53.0 1.1 %convolution_add_fusion.6 = f32[128,384]{1,0:T(8,128)S(1)} fusion(f32[128,384]{1,0:T(8,128)S(1)} %convolution_add_fusion.7, bf16[128,384]{1,0:T(8,128)(2,1)} %bitcast.412, bf16[9,384,384]{2,1,0:T(8,128)(2,1)S(1)} %copy-done.2), kind=kOutput, calls=%fused_computation.58 | convolution fusion | flops 37797888 | bytes 786432 | tf_op jit(solution)/shard_map/dot_general | solution.py:78
  54.1 1.1 %convolution_add_fusion.5 = f32[128,384]{1,0:T(8,128)S(1)} fusion(f32[128,384]{1,0:T(8,128)S(1)} %convolution_add_fusion.6, bf16[128,384]{1,0:T(8,128)(2,1)} %bitcast.411, bf16[9,384,384]{2,1,0:T(8,128)(2,1)S(1)} %copy-done.2), kind=kOutput, calls=%fused_computation.57 | convolution fusion | flops 37797888 | bytes 786432 | tf_op jit(solution)/shard_map/dot_general | solution.py:78
  55.2 1.1 %convolution_add_fusion.4 = f32[128,384]{1,0:T(8,128)S(1)} fusion(f32[128,384]{1,0:T(8,128)S(1)} %convolution_add_fusion.5, bf16[128,384]{1,0:T(8,128)(2,1)} %bitcast.410, bf16[9,384,384]{2,1,0:T(8,128)(2,1)S(1)} %copy-done.2), kind=kOutput, calls=%fused_computation.56 | convolution fusion | flops 37797888 | bytes 786432 | tf_op jit(solution)/shard_map/dot_general | solution.py:78
  56.3 1.1 %convolution_add_fusion.3 = f32[128,384]{1,0:T(8,128)S(1)} fusion(f32[128,384]{1,0:T(8,128)S(1)} %convolution_add_fusion.4, bf16[128,384]{1,0:T(8,128)(2,1)} %bitcast.409, bf16[9,384,384]{2,1,0:T(8,128)(2,1)S(1)} %copy-done.2), kind=kOutput, calls=%fused_computation.55 | convolution fusion | flops 37797888 | bytes 786432 | tf_op jit(solution)/shard_map/dot_general | solution.py:78
  57.5 0.2 convolution_add_fusion.2
  57.7 0.2 convolution_add_fusion.1
  57.9 0.2 fusion.3
  58.2 3.1 %collective-permute-start.1 = (bf16[1,2,8,384]{3,2,1,0:T(8,128)(2,1)S(1)}, bf16[1,2,8,384]{3,2,1,0:T(8,128)(2,1)S(1)}, u32[]{:S(2)}, u32[]{:S(2)}) collective-permute-start(bf16[1,2,8,384]{3,2,1,0:T(8,128)(2,1)S(1)} %constant_dynamic-slice_fusion), channel_id=1, source_target_pairs={{0,2},{2,4},{4,6},{6,8},{8,10},{10,12},{12,14},{14,16},{16,18},{18... | collective-permute-start | bytes 36872 | tf_op jit(solution)/shard_map/ppermute | solution.py:12
  61.5 3.0 %collective-permute-done.1 = bf16[1,2,8,384]{3,2,1,0:T(8,128)(2,1)S(1)} collective-permute-done((bf16[1,2,8,384]{3,2,1,0:T(8,128)(2,1)S(1)}, bf16[1,2,8,384]{3,2,1,0:T(8,128)(2,1)S(1)}, u32[]{:S(2)}, u32[]{:S(2)}) %collective-permute-start.1) | collective-permute-done | bytes 12320 | tf_op jit(solution)/shard_map/ppermute | solution.py:12
  64.8 0.3 multiply_reduce_fusion.1
  65.3 2.2 %collective-permute-start.2 = (bf16[2,2,8,384]{3,2,1,0:T(8,128)(2,1)S(1)}, bf16[2,2,8,384]{3,2,1,0:T(8,128)(2,1)S(1)}, u32[]{:S(2)}, u32[]{:S(2)}) collective-permute-start(bf16[2,2,8,384]{3,2,1,0:T(8,128)(2,1)S(1)} %pad_dynamic-slice_fusion.1), channel_id=1, source_target_pairs={{0,2},{2,4},{4,6},{6,8},{8,10},{10,12},{12,14},{14,16},{16,18},{18... | collective-permute-start | bytes 73736 | tf_op jit(solution)/shard_map/ppermute | solution.py:12
  67.5 4.4 %collective-permute-done.2 = bf16[2,2,8,384]{3,2,1,0:T(8,128)(2,1)S(1)} collective-permute-done((bf16[2,2,8,384]{3,2,1,0:T(8,128)(2,1)S(1)}, bf16[2,2,8,384]{3,2,1,0:T(8,128)(2,1)S(1)}, u32[]{:S(2)}, u32[]{:S(2)}) %collective-permute-start.2) | collective-permute-done | bytes 24608 | tf_op jit(solution)/shard_map/ppermute | solution.py:12
  72.0 3.1 %all_gather.6 = bf16[6,4,8,384]{3,2,1,0:T(8,128)(2,1)S(1)} all-gather(bf16[6,2,8,384]{3,2,1,0:T(8,128)(2,1)S(1)} %pad_maximum_fusion.1), channel_id=1, replica_groups=mesh['frames'=16,'rows'=2] {'rows'}, dimensions={1}, use_global_device_ids=true | all-gather | bytes 221184 | tf_op jit(solution)/shard_map/all_gather | solution.py:109
  75.2 0.2 pad_slice_fusion.24
  75.4 1.1 %fusion.86 = f32[128,192]{0,1:T(8,128)S(1)} fusion(bf16[128,384]{1,0:T(8,128)(2,1)S(1)} %bitcast.406, bf16[27,192,384]{2,1,0:T(8,128)(2,1)} %param.19), kind=kOutput, calls=%fused_computation.197 | convolution fusion | flops 18874368 | bytes 344064 | tf_op jit(solution)/shard_map/dot_general | solution.py:29
  76.7 0.2 convolution_add_fusion.58
  77.0 0.2 convolution_add_fusion.57
  77.4 0.2 convolution_add_fusion.55
  77.6 0.2 convolution_add_fusion.54
  78.0 0.2 convolution_add_fusion.52
  78.2 0.2 convolution_add_fusion.51
  79.1 0.2 convolution_add_fusion.47
  79.3 0.2 convolution_add_fusion.46
  79.7 0.2 convolution_add_fusion.44
  79.9 0.2 convolution_add_fusion.43
  80.3 0.2 convolution_add_fusion.41
  80.6 0.2 convolution_add_fusion.40
  81.0 0.2 convolution_add_fusion.38
  81.2 0.2 convolution_add_fusion.37
  81.6 0.2 convolution_add_fusion.35
  81.8 0.2 convolution_add_fusion.34
  82.2 3.8 %all_to_all.8 = bf16[4,4,8,192]{3,2,0,1:T(8,128)(2,1)S(1)} all-to-all(bf16[4,4,8,192]{3,2,0,1:T(8,128)(2,1)S(1)} %copy.26), channel_id=1, replica_groups=mesh['frames'=16,'rows'=2] {'rows'}, dimensions={1} | all-to-all | bytes 98304 | tf_op jit(solution)/shard_map/all_to_all | solution.py:116
  86.5 2.2 %collective-permute-start.3 = (bf16[2,2,8,384]{3,2,1,0:T(8,128)(2,1)S(1)}, bf16[2,2,8,384]{3,2,1,0:T(8,128)(2,1)S(1)}, u32[]{:S(2)}, u32[]{:S(2)}) collective-permute-start(bf16[2,2,8,384]{3,2,1,0:T(8,128)(2,1)S(1)} %pad_dynamic-slice_fusion), channel_id=1, source_target_pairs={{0,2},{2,4},{4,6},{6,8},{8,10},{10,12},{12,14},{14,16},{16,18},{18... | collective-permute-start | bytes 73736 | tf_op jit(solution)/shard_map/ppermute | solution.py:12
  88.7 4.4 %collective-permute-done.3 = bf16[2,2,8,384]{3,2,1,0:T(8,128)(2,1)S(1)} collective-permute-done((bf16[2,2,8,384]{3,2,1,0:T(8,128)(2,1)S(1)}, bf16[2,2,8,384]{3,2,1,0:T(8,128)(2,1)S(1)}, u32[]{:S(2)}, u32[]{:S(2)}) %collective-permute-start.3) | collective-permute-done | bytes 24608 | tf_op jit(solution)/shard_map/ppermute | solution.py:12
  93.2 3.1 %all_gather.7 = bf16[6,4,8,384]{3,2,1,0:T(8,128)(2,1)S(1)} all-gather(bf16[6,2,8,384]{3,2,1,0:T(8,128)(2,1)S(1)} %pad_maximum_fusion.2), channel_id=1, replica_groups=mesh['frames'=16,'rows'=2] {'rows'}, dimensions={1}, use_global_device_ids=true | all-gather | bytes 221184 | tf_op jit(solution)/shard_map/all_gather | solution.py:121
  96.3 0.2 pad_slice_fusion
  96.6 1.1 %fusion.58 = f32[128,192]{0,1:T(8,128)S(1)} fusion(bf16[128,384]{1,0:T(8,128)(2,1)S(1)} %bitcast.407, bf16[27,192,384]{2,1,0:T(8,128)(2,1)} %param.22), kind=kOutput, calls=%fused_computation.169 | convolution fusion | flops 18874368 | bytes 344064 | tf_op jit(solution)/shard_map/dot_general | solution.py:29
  97.9 0.2 convolution_add_fusion.32
  98.3 0.2 convolution_add_fusion.30
  98.5 0.2 convolution_add_fusion.29
  98.9 0.2 convolution_add_fusion.27
  99.1 0.2 convolution_add_fusion.26
  100.0 0.2 convolution_add_fusion.22
  100.6 0.2 convolution_add_fusion.19
  101.3 0.2 convolution_add_fusion.16
  101.9 0.2 convolution_add_fusion.13
  102.5 0.2 convolution_add_fusion.10
  103.3 3.8 %all_to_all.9 = bf16[4,4,8,192]{3,2,0,1:T(8,128)(2,1)S(1)} all-to-all(bf16[4,4,8,192]{3,2,0,1:T(8,128)(2,1)S(1)} %copy.30), channel_id=1, replica_groups=mesh['frames'=16,'rows'=2] {'rows'}, dimensions={1} | all-to-all | bytes 98304 | tf_op jit(solution)/shard_map/all_to_all | solution.py:127
  107.4 0.7 fusion.150
  (87 shorter events, 7.3 us)
Async XLA Ops:
  0.0 51.9 %copy-start.2 = (bf16[9,384,384]{2,1,0:T(8,128)(2,1)S(1)}, bf16[9,384,384]{2,1,0:T(8,128)(2,1)}, u32[]{:S(2)}) copy-start(bf16[9,384,384]{2,1,0:T(8,128)(2,1)} %param.14) | copy-start | bytes 7962628
  1.1 8.0 %collective-permute-start = (bf16[8,1,16,384]{3,2,1,0:T(8,128)(2,1)S(1)}, bf16[8,1,16,384]{3,2,1,0:T(8,128)(2,1)S(1)}, u32[]{:S(2)}, u32[]{:S(2)}) collective-permute-start(bf16[8,1,16,384]{3,2,1,0:T(8,128)(2,1)S(1)} %slice.409), channel_id=1, source_target_pairs={{1,0},{3,2},{5,4},{7,6},{9,8},{11,10},{13,12},{15,14},{17,16},{19,... | collective-permute-start | bytes 294920 | tf_op jit(solution)/shard_map/ppermute | solution.py:12
  10.1 47.8 %copy-start.6 = (f32[384]{0:T(512)S(1)}, f32[384]{0:T(512)}, u32[]{:S(2)}) copy-start(f32[384]{0:T(512)} %param.15) | copy-start | bytes 4612
  50.6 6.9 %copy-start.3 = (bf16[8,2,8,384]{3,2,1,0:T(8,128)(2,1)S(1)}, bf16[8,2,8,384]{3,2,1,0:T(8,128)(2,1)}, u32[]{:S(2)}) copy-start(bf16[8,2,8,384]{3,2,1,0:T(8,128)(2,1)} %slice.422) | copy-start | bytes 294916
  50.6 7.4 %copy-start.5 = (bf16[8,2,8,384]{3,2,1,0:T(8,128)(2,1)S(1)}, bf16[8,2,8,384]{3,2,1,0:T(8,128)(2,1)}, u32[]{:S(2)}) copy-start(bf16[8,2,8,384]{3,2,1,0:T(8,128)(2,1)} %slice.426) | copy-start | bytes 294916
  50.6 10.7 %copy-start.4 = (bf16[3,384,384]{2,1,0:T(8,128)(2,1)S(1)}, bf16[3,384,384]{2,1,0:T(8,128)(2,1)}, u32[]{:S(2)}) copy-start(bf16[3,384,384]{2,1,0:T(8,128)(2,1)} %param.16) | copy-start | bytes 2654212
  51.9 12.9 %copy-start.11 = (f32[384]{0:T(512)S(1)}, f32[384]{0:T(512)}, u32[]{:S(2)}) copy-start(f32[384]{0:T(512)} %param.17) | copy-start | bytes 4612
  53.0 12.2 %copy-start.7 = (f32[384]{0:T(512)S(1)}, f32[384]{0:T(512)}, u32[]{:S(2)}) copy-start(f32[384]{0:T(512)} %param.18) | copy-start | bytes 4612
  58.2 6.4 %collective-permute-start.1 = (bf16[1,2,8,384]{3,2,1,0:T(8,128)(2,1)S(1)}, bf16[1,2,8,384]{3,2,1,0:T(8,128)(2,1)S(1)}, u32[]{:S(2)}, u32[]{:S(2)}) collective-permute-start(bf16[1,2,8,384]{3,2,1,0:T(8,128)(2,1)S(1)} %constant_dynamic-slice_fusion), channel_id=1, source_target_pairs={{0,2},{2,4},{4,6},{6,8},{8,10},{10,12},{12,14},{14,16},{16,18},{18... | collective-permute-start | bytes 36872 | tf_op jit(solution)/shard_map/ppermute | solution.py:12
  65.2 11.4 %copy-start = (bf16[27,192,384]{2,1,0:T(8,128)(2,1)S(1)}, bf16[27,192,384]{2,1,0:T(8,128)(2,1)}, u32[]{:S(2)}) copy-start(bf16[27,192,384]{2,1,0:T(8,128)(2,1)} %param.19) | copy-start | bytes 11943940
  65.3 6.6 %collective-permute-start.2 = (bf16[2,2,8,384]{3,2,1,0:T(8,128)(2,1)S(1)}, bf16[2,2,8,384]{3,2,1,0:T(8,128)(2,1)S(1)}, u32[]{:S(2)}, u32[]{:S(2)}) collective-permute-start(bf16[2,2,8,384]{3,2,1,0:T(8,128)(2,1)S(1)} %pad_dynamic-slice_fusion.1), channel_id=1, source_target_pairs={{0,2},{2,4},{4,6},{6,8},{8,10},{10,12},{12,14},{14,16},{16,18},{18... | collective-permute-start | bytes 73736 | tf_op jit(solution)/shard_map/ppermute | solution.py:12
  78.4 3.7 %copy-start.9 = (f32[192]{0:T(256)S(1)}, f32[192]{0:T(256)}, u32[]{:S(2)}) copy-start(f32[192]{0:T(256)} %param.20) | copy-start | bytes 2308
  78.9 7.5 %copy-start.8 = (f32[384]{0:T(512)S(1)}, f32[384]{0:T(512)}, u32[]{:S(2)}) copy-start(f32[384]{0:T(512)} %param.21) | copy-start | bytes 4612
  86.4 11.3 %copy-start.1 = (bf16[27,192,384]{2,1,0:T(8,128)(2,1)S(1)}, bf16[27,192,384]{2,1,0:T(8,128)(2,1)}, u32[]{:S(2)}) copy-start(bf16[27,192,384]{2,1,0:T(8,128)(2,1)} %param.22) | copy-start | bytes 11943940
  86.5 6.6 %collective-permute-start.3 = (bf16[2,2,8,384]{3,2,1,0:T(8,128)(2,1)S(1)}, bf16[2,2,8,384]{3,2,1,0:T(8,128)(2,1)S(1)}, u32[]{:S(2)}, u32[]{:S(2)}) collective-permute-start(bf16[2,2,8,384]{3,2,1,0:T(8,128)(2,1)S(1)} %pad_dynamic-slice_fusion), channel_id=1, source_target_pairs={{0,2},{2,4},{4,6},{6,8},{8,10},{10,12},{12,14},{14,16},{16,18},{18... | collective-permute-start | bytes 73736 | tf_op jit(solution)/shard_map/ppermute | solution.py:12
  99.6 3.7 %copy-start.10 = (f32[192]{0:T(256)S(1)}, f32[192]{0:T(256)}, u32[]{:S(2)}) copy-start(f32[192]{0:T(256)} %param.23) | copy-start | bytes 2308
where the time goes:
time: 109 us; the launch traced here: 108 us
  local copies, waits for them, and re-layouts  43.2 us (40%)
  matrix products  20.9 us (19%)
  blocking collectives  13.8 us (13%)
  waiting for transfers between devices  11.9 us (11%)
  starting transfers between devices  10.1 us (9%)
  between operations  4.74 us (4%)
  other arithmetic  3.51 us (3%)
    slice x9, local copies, waits for them, and re-layouts, per_device(): extended[:, tap_r:tap_r + 2 * out_rows:2, tap_c:tap_c + 2 * out_cols:2]  40.4 us
    dot_general x54, matrix products, conv_taps(): lax.dot_general(flat_rows, weight[tap_t * 9 + tap_r * 3 + tap_c], (((1,),...  12.8 us
    ppermute x4, waiting for transfers between devices, shifted(): lax.ppermute(value, axis, [(source, source + steps) for source in range(i...  11.9 us
    ppermute x4, starting transfers between devices, shifted(): lax.ppermute(value, axis, [(source, source + steps) for source in range(i...  10.1 us
    dot_general x9, matrix products, per_device(): jnp.dot(window.reshape(-1, channels), down_weight[tap_r * 3 + tap_c], pre...  7.44 us
    all_to_all x1, blocking collectives, per_device(): lax.all_to_all(part_one, 'rows', split_axis=1, concat_axis=3, tiled=True)  3.8 us
    all_to_all x1, blocking collectives, per_device(): lax.all_to_all(part_two, 'rows', split_axis=1, concat_axis=3, tiled=True)  3.8 us
    all_gather x1, blocking collectives, per_device(): lax.all_gather(jnp.concatenate([prior_one, act_one], axis=0), 'rows', axi...  3.1 us
  transfers between devices with their start and end apart: 4, of which 3 were waited for; matrix products, arithmetic and copies ran while one was open for 2% of the time, Pallas kernels for 0%

commit v1 on v0

v1 whole, which is shorter than its diff:
```python
import functools

import jax
import jax.numpy as jnp
from jax import lax
from jax.experimental import pallas as pl
from jax.experimental.pallas import tpu as pltpu
from jax.sharding import PartitionSpec as P

MESH = pl.DeviceIdType.MESH
F32 = jnp.float32
BF16 = jnp.bfloat16
EPSILON = 1e-06
LANES = 128
LEFT = 8


def rms_silu(values, gain):
    mean_sq = jnp.mean(values * values, axis=-1, keepdims=True)
    return jax.nn.silu(values * lax.rsqrt(mean_sq + EPSILON) * gain)


def round16(values):
    return values.astype(BF16).astype(F32)


def join(row, own, other):
    low = jnp.where(row == 0, own, other)
    high = jnp.where(row == 0, other, own)
    return jnp.concatenate([low, high], axis=-1)


def dot_t(values, weight):
    return lax.dot_general(values, weight, (((1,), (1,)), ((), ())), preferred_element_type=F32)


def kernel(
    shards,
    video,
    counts,
    down_weight,
    spatial_bias,
    time_weight,
    time_bias,
    gain1,
    weight1,
    bias1,
    gain2,
    weight2,
    bias2,
    out,
    vid_v,
    halo_v,
    down_v,
    time_v,
    w1_v,
    w2_v,
    xf,
    xs,
    timeline,
    red_own,
    red_other,
    last_red,
    before_v,
    lat_v,
    padded,
    patches,
    last_act,
    prior_act,
    hid,
    h_own,
    h_other,
    h_last,
    h_prior,
    h2_send,
    h2_recv,
    in_sem,
    down_sem,
    w1_sem,
    w2_sem,
    send_sem,
    recv_sem,
    before_sem,
    prior_sem,
):
    shard = lax.axis_index("frames")
    row = lax.axis_index("rows")
    other = 1 - row
    slots, in_rows, in_cols, chans = vid_v.shape
    out_slots, own_rows, cols = slots // 2, in_rows // 2, in_cols // 2
    all_rows = 2 * own_rows
    half = h_own.shape[1]
    plane = all_rows * cols
    has_next = shard < shards - 1
    has_prev = shard > 0

    vid_copy = pltpu.make_async_copy(video, vid_v, in_sem.at[0])
    vid_copy.start()
    down_copies = []
    for k in range(3):
        copy = pltpu.make_async_copy(
            down_weight.at[pl.ds(3 * k, 3)], down_v.at[pl.ds(3 * k, 3)], down_sem.at[k]
        )
        copy.start()
        down_copies.append(copy)

    barrier = pltpu.get_barrier_semaphore()
    pl.semaphore_signal(barrier, inc=1, device_id=(shard, other), device_id_type=MESH)

    @pl.when(has_next)
    def _():
        for r in range(2):
            pl.semaphore_signal(barrier, inc=1, device_id=(shard + 1, r), device_id_type=MESH)

    @pl.when(has_prev)
    def _():
        for r in range(2):
            pl.semaphore_signal(barrier, inc=1, device_id=(shard - 1, r), device_id_type=MESH)

    time_copy = pltpu.make_async_copy(time_weight, time_v, in_sem.at[1])
    time_copy.start()

    def start_weight(source, target, sems):
        copies = {}
        for kt in (2, 1, 0):
            for tap in range(9 * kt, 9 * kt + 9):
                copies[tap] = pltpu.make_async_copy(
                    source.at[tap], target.at[:, pl.ds(tap * chans, chans)], sems.at[tap]
                )
                copies[tap].start()
        return copies

    w1_copies = start_weight(weight1, w1_v, w1_sem)
    w2_copies = start_weight(weight2, w2_v, w2_sem)

    own_count = counts[shard]
    live = jnp.where(shard == 0, 1, own_count // 2)

    pl.semaphore_wait(
        barrier, 1 + jnp.where(has_next, 2, 0) + jnp.where(has_prev, 2, 0)
    )

    def remote(source, target, index, device, recv=None):
        return pltpu.make_async_remote_copy(
            src_ref=source,
            dst_ref=target,
            send_sem=send_sem.at[index],
            recv_sem=recv_sem.at[index] if recv is None else recv,
            device_id=device,
            device_id_type=MESH,
        )

    halo_copy = remote(video.at[:, 0], halo_v, 0, (shard, other))

    @pl.when(row == 1)
    def _():
        halo_copy.start()
        halo_v[...] = jnp.zeros_like(halo_v)

    padded[...] = jnp.zeros_like(padded)
    hid[0:2] = jnp.zeros((2,) + hid.shape[1:], F32)
    xf[:, :, :, in_cols:] = jnp.zeros(xf.shape[:3] + (xf.shape[3] - in_cols, LANES), F32)

    def spread(line, values):
        values = values.astype(F32)
        for lanes in range(chans // LANES):
            begin = lanes * LANES
            xf[line, lanes, :, 0:in_cols] = values[:, :, begin : begin + LANES]
            for tc in range(3):
                part = xf[line, lanes, :, pl.ds(tc, cols, stride=2), :]
                at = tc * chans + begin
                xs[line, :, at : at + LANES] = part.reshape(slots * cols, LANES).astype(BF16)

    vid_copy.wait()
    for line in range(in_rows):
        spread(line, vid_v[:, line])

    total = None
    for tr in range(3):
        if tr == 2:

            @pl.when(row == 0)
            def _():
                halo_copy.wait_recv()

            spread(in_rows, halo_v[...])
        down_copies[tr].wait()
        lines = jnp.concatenate([xs[2 * r + tr] for r in range(own_rows)], axis=0)
        taps = down_v[3 * tr : 3 * tr + 3].reshape(3 * chans, chans)
        part = jnp.dot(lines, taps, preferred_element_type=F32)
        total = part if total is None else total + part
    reduced = (total + spatial_bias[...]).astype(BF16)
    red_own[...] = reduced
    red_copy = remote(red_own, red_other, 1, (shard, other))
    red_copy.start()

    def to_timeline(values, first_row):
        values = values.astype(F32).reshape(own_rows, slots, cols, chans)
        for f in range(slots):
            timeline[f + 1, pl.ds(first_row, own_rows)] = values[:, f]

    to_timeline(reduced, own_rows * row)
    last_red[...] = (
        timeline[own_count, pl.ds(own_rows * row, own_rows)].reshape(own_rows * cols, chans).astype(BF16)
    )
    before_copies = [
        remote(last_red, before_v.at[row], 2 + r, (shard + 1, r), before_sem.at[row]) for r in range(2)
    ]

    def next_start(copies):
        @pl.when(has_next)
        def _():
            for copy in copies:
                copy.start()

    def prev_wait(copies, buffer):
        @pl.when(has_prev)
        def _():
            for copy in copies:
                copy.wait_recv()

        @pl.when(jnp.logical_not(has_prev))
        def _():
            buffer[...] = jnp.zeros_like(buffer)

    next_start(before_copies)
    before_waits = [
        remote(last_red, before_v.at[r], 2, (shard, other), before_sem.at[r]) for r in range(2)
    ]

    red_copy.wait_recv()
    to_timeline(red_other[...], own_rows * other)
    time_copy.wait()

    def tap_frames(kt):
        frames = [timeline[2 * t + kt].reshape(plane, chans) for t in range(out_slots)]
        return jnp.concatenate(frames, axis=0).astype(BF16)

    merged = None
    for kt in (2, 1, 0):
        if kt == 0:
            prev_wait(before_waits, before_v)
            timeline[0] = before_v[...].astype(F32).reshape(all_rows, cols, chans)
        part = jnp.dot(tap_frames(kt), time_v[kt], preferred_element_type=F32)
        merged = part if merged is None else merged + part
    merged = merged + time_bias[...]
    first = jnp.where(shard == 0, timeline[1].reshape(plane, chans), merged[:plane])
    latent = round16(jnp.concatenate([first, merged[plane:]], axis=0))
    lat_v[...] = latent.reshape(lat_v.shape)

    def place(first_frame, frames, values):
        padded[first_frame : first_frame + frames, 1 : 1 + all_rows, LEFT : LEFT + cols, :] = values.reshape(
            frames, all_rows, cols, chans
        )
        for kj in range(3):
            begin = LEFT - 1 + kj
            window = padded[first_frame : first_frame + frames, :, begin : begin + cols, :]
            for ki in range(3):
                tap = 3 * ki + kj
                patches[first_frame : first_frame + frames, :, tap * chans : (tap + 1) * chans] = (
                    window[:, ki : ki + all_rows].reshape(frames, plane, chans).astype(BF16)
                )

    def conv_part(kt, target, copies):
        for tap in range(9 * kt, 9 * kt + 9):
            copies[tap].wait()
        lines = patches[kt : kt + out_slots].reshape(out_slots * plane, 9 * chans)
        return dot_t(lines, target[:, 9 * kt * chans : 9 * (kt + 1) * chans])

    act_one = round16(rms_silu(latent, gain1[...]))
    place(2, out_slots, act_one)
    recent = padded[pl.ds(live, 2), 1 : 1 + all_rows, LEFT : LEFT + cols, :]
    last_act[...] = recent.reshape(2 * plane, chans).astype(BF16)
    act_copy = remote(last_act, prior_act, 4, (shard + 1, row))
    next_start([act_copy])
    acc = conv_part(2, w1_v, w1_copies)
    prev_wait([act_copy], prior_act)
    place(0, 2, prior_act[...].astype(F32))
    for kt in (1, 0):
        acc = acc + conv_part(kt, w1_v, w1_copies)
    part_one = (acc + bias1[...]).astype(BF16)
    h_own[...] = part_one
    h_copy = remote(h_own, h_other, 5, (shard, other))
    h_copy.start()
    hid[2 : 2 + out_slots] = part_one.astype(F32).reshape(out_slots, plane, half)
    h_last[...] = hid[pl.ds(live, 2)].reshape(2 * plane, half).astype(BF16)
    prior_copies = [
        remote(h_last, h_prior.at[row], 6 + r, (shard + 1, r), prior_sem.at[row]) for r in range(2)
    ]
    next_start(prior_copies)
    prior_waits = [
        remote(h_last, h_prior.at[r], 6, (shard, other), prior_sem.at[r]) for r in range(2)
    ]

    h_copy.wait_recv()
    hidden = join(row, part_one.astype(F32), h_other[...].astype(F32))
    place(2, out_slots, rms_silu(hidden, gain2[...]))
    acc = conv_part(2, w2_v, w2_copies)
    prev_wait(prior_waits, h_prior)
    hidden = jnp.concatenate([h_prior[0].astype(F32), h_prior[1].astype(F32)], axis=-1)
    place(0, 2, rms_silu(hidden, gain2[...]))
    for kt in (1, 0):
        acc = acc + conv_part(kt, w2_v, w2_copies)
    part_two = round16(acc + bias2[...]).reshape(out_slots, plane, half)
    hid[2 : 2 + out_slots] = part_two
    rows_of = own_rows * cols

    def share(which):
        return hid[2 : 2 + out_slots, pl.ds(which * rows_of, rows_of)].reshape(out_slots * rows_of, half)

    h2_send[...] = share(other).astype(BF16)
    h2_copy = remote(h2_send, h2_recv, 8, (shard, other))
    h2_copy.start()
    mine = share(row)
    kept = lat_v[:, pl.ds(own_rows * row, own_rows)]

    @pl.when(has_next)
    def _():
        for copy in before_copies + [act_copy] + prior_copies:
            copy.wait_send()

    @pl.when(row == 1)
    def _():
        halo_copy.wait_send()

    red_copy.wait_send()
    h_copy.wait_send()
    h2_copy.wait_recv()
    hidden = join(row, mine, h2_recv[...].astype(F32)).reshape(out_slots, own_rows, cols, chans)
    slot = lax.broadcasted_iota(jnp.int32, hidden.shape, 0)
    out[...] = jnp.where(slot < live, kept + hidden, 0.0).astype(out.dtype)
    h2_copy.wait_send()


def per_device(shards, video, counts, down, sbias, time, tbias, gain1, w1, b1, gain2, w2, b2):
    slots, in_rows, in_cols, chans = video.shape
    out_slots, own_rows, cols = slots // 2, in_rows // 2, in_cols // 2
    all_rows = 2 * own_rows
    half = w1.shape[1]
    plane = all_rows * cols
    hbm = pl.BlockSpec(memory_space=pl.ANY)
    vmem = pl.BlockSpec(memory_space=pltpu.VMEM)
    smem = pl.BlockSpec(memory_space=pltpu.SMEM)
    dma = pltpu.SemaphoreType.DMA
    return pl.pallas_call(
        functools.partial(kernel, shards),
        out_shape=jax.ShapeDtypeStruct((out_slots, own_rows, cols, chans), BF16),
        in_specs=[hbm, smem, hbm, vmem, hbm, vmem, vmem, hbm, vmem, vmem, hbm, vmem],
        out_specs=vmem,
        scratch_shapes=[
            pltpu.VMEM(video.shape, BF16),
            pltpu.VMEM((slots, in_cols, chans), BF16),
            pltpu.VMEM(down.shape, BF16),
            pltpu.VMEM(time.shape, BF16),
            pltpu.VMEM((half, 27 * chans), BF16),
            pltpu.VMEM((half, 27 * chans), BF16),
            pltpu.VMEM((in_rows + 1, chans // LANES, slots, in_cols + 8, LANES), F32),
            pltpu.VMEM((in_rows + 1, slots * cols, 3 * chans), BF16),
            pltpu.VMEM((slots + 1, all_rows, cols, chans), F32),
            pltpu.VMEM((own_rows * slots * cols, chans), BF16),
            pltpu.VMEM((own_rows * slots * cols, chans), BF16),
            pltpu.VMEM((own_rows * cols, chans), BF16),
            pltpu.VMEM((2, own_rows * cols, chans), BF16),
            pltpu.VMEM((out_slots, all_rows, cols, chans), F32),
            pltpu.VMEM((2 + out_slots, all_rows + 2, cols + 16, chans), F32),
            pltpu.VMEM((2 + out_slots, plane, 9 * chans), BF16),
            pltpu.VMEM((2 * plane, chans), BF16),
            pltpu.VMEM((2 * plane, chans), BF16),
            pltpu.VMEM((2 + out_slots, plane, half), F32),
            pltpu.VMEM((out_slots * plane, half), BF16),
            pltpu.VMEM((out_slots * plane, half), BF16),
            pltpu.VMEM((2 * plane, half), BF16),
            pltpu.VMEM((2, 2 * plane, half), BF16),
            pltpu.VMEM((out_slots * own_rows * cols, half), BF16),
            pltpu.VMEM((out_slots * own_rows * cols, half), BF16),
            dma((2,)),
            dma((3,)),
            dma((27,)),
            dma((27,)),
            dma((9,)),
            dma((9,)),
            dma((2,)),
            dma((2,)),
        ],
        compiler_params=pltpu.CompilerParams(
            collective_id=0, has_side_effects=True, vmem_limit_bytes=48 * 1024 * 1024
        ),
        name="section",
    )(
        video,
        counts,
        down,
        sbias.reshape(1, -1),
        time,
        tbias.reshape(1, -1),
        gain1.reshape(1, -1),
        w1,
        b1.reshape(1, -1),
        gain2.reshape(1, -1),
        w2,
        b2.reshape(1, -1),
    )


def solution(mesh):
    in_specs = (
        P("frames", "rows", None, None),
        P(),
        P(),
        P(),
        P(),
        P(),
        P(),
        P(None, "rows", None),
        P("rows"),
        P(),
        P(None, "rows", None),
        P("rows"),
    )
    return jax.shard_map(
        functools.partial(per_device, mesh.shape["frames"]),
        mesh=mesh,
        in_specs=in_specs,
        out_specs=P("frames", "rows", None, None),
        check_vma=False,
    )
```

time: 109 us -> 31.6 us (0.29)
  local copies, waits for them, and re-layouts: 43.2 us -> 9.28 us
  Pallas kernels: 0 us -> 21.9 us
  matrix products: 20.9 us -> 0 us
  blocking collectives: 13.8 us -> 0 us
  waiting for transfers between devices: 11.9 us -> 0 us
  starting transfers between devices: 10.1 us -> 0 us
  between operations: 4.74 us -> 0.02 us
  other arithmetic: 3.51 us -> 0 us
    slice x17 -> x0, local copies, waits for them, and re-layouts: 42.1 us -> none  [the longest x9 40.4 us: per_device(): extended[:, tap_r:tap_r + 2 * out_rows:2, tap_c:tap_c + 2 * out_cols:2]]
    pallas_call x0 -> x1, Pallas kernels: none -> 21.9 us  [per_device(): pl.pallas_call(functools.partial(kernel, shards), out_shape=jax.ShapeDtyp...]
    dot_general x66 -> x0, matrix products: 20.9 us -> none  [the longest x54 12.8 us: conv_taps(): lax.dot_general(flat_rows, weight[tap_t * 9 + tap_r * 3 + tap_c], (((1,),...]
    ppermute x4 -> x0, waiting for transfers between devices: 11.9 us -> none  [shifted(): lax.ppermute(value, axis, [(source, source + steps) for source in range(i...]
    ppermute x4 -> x0, starting transfers between devices: 10.1 us -> none  [shifted(): lax.ppermute(value, axis, [(source, source + steps) for source in range(i...]
    all_to_all x2 -> x0, blocking collectives: 7.59 us -> none  [the longest x1 3.8 us: per_device(): lax.all_to_all(part_one, 'rows', split_axis=1, concat_axis=3, tiled=True)]
    unnamed x24 -> x13, local copies, waits for them, and re-layouts: 0.07 us -> 6.55 us
    all_gather x2 -> x0, blocking collectives: 6.16 us -> none  [the longest x1 3.1 us: per_device(): lax.all_gather(jnp.concatenate([prior_one, act_one], axis=0), 'rows', axi...]
  transfers between devices with their start and end apart: 4 -> 0, of which waited for: 3 -> 0; matrix products, arithmetic and copies ran while one was open for 2% -> 0% of each run, Pallas kernels for 0% -> 0%
where the time goes in v1:
time: 31.6 us; the launch traced here: 31.2 us
  Pallas kernels  21.9 us (69%)
  local copies, waits for them, and re-layouts  9.28 us (29%)
    pallas_call x1, Pallas kernels, per_device(): pl.pallas_call(functools.partial(kernel, shards), out_shape=jax.ShapeDtyp...  21.9 us
    unnamed x13, local copies, waits for them, and re-layouts  6.55 us
    reshape x1, local copies, waits for them, and re-layouts, per_device(): tbias.reshape(1, -1)  0.68 us
    reshape x1, local copies, waits for them, and re-layouts, per_device(): gain1.reshape(1, -1)  0.68 us
    reshape x1, local copies, waits for them, and re-layouts, per_device(): gain2.reshape(1, -1)  0.68 us
    reshape x1, local copies, waits for them, and re-layouts, per_device(): sbias.reshape(1, -1)  0.68 us

profile of v1, /device:TPU:25, one launch (start us, length us, event | category | flops | bytes accessed | tf_op | source)
XLA Modules:
  0.0 31.2 jit_solution(9045357398242886332)
XLA Ops:
  0.0 0.7 %reshape.18.spatial_bias = f32[1,384]{1,0:T(1,128)S(1)} reshape(f32[384]{0:T(512)} %param.15) | data formatting | bytes 3072 | tf_op jit(solution)/shard_map/reshape | solution.py:393
  0.7 0.7 %reshape.19.time_bias = f32[1,384]{1,0:T(1,128)S(1)} reshape(f32[384]{0:T(512)} %param.17) | data formatting | bytes 3072 | tf_op jit(solution)/shard_map/reshape | solution.py:395
  1.4 0.7 %reshape.20.gain1 = f32[1,384]{1,0:T(1,128)S(1)} reshape(f32[384]{0:T(512)} %param.18) | data formatting | bytes 3072 | tf_op jit(solution)/shard_map/reshape | solution.py:396
  2.0 0.7 %reshape.22.gain2 = f32[1,384]{1,0:T(1,128)S(1)} reshape(f32[384]{0:T(512)} %param.21) | data formatting | bytes 3072 | tf_op jit(solution)/shard_map/reshape | solution.py:399
  2.7 0.0 copy-start
  2.7 1.7 %copy-done = bf16[9,384,384]{2,1,0:T(8,128)(2,1)S(1)} copy-done((bf16[9,384,384]{2,1,0:T(8,128)(2,1)S(1)}, bf16[9,384,384]{2,1,0:T(8,128)(2,1)}, u32[]{:S(2)}) %copy-start) | copy-done | bytes 2654232
  4.5 0.0 copy-start.1
  4.5 1.2 %copy-done.1 = bf16[3,384,384]{2,1,0:T(8,128)(2,1)S(1)} copy-done((bf16[3,384,384]{2,1,0:T(8,128)(2,1)S(1)}, bf16[3,384,384]{2,1,0:T(8,128)(2,1)}, u32[]{:S(2)}) %copy-start.1) | copy-done | bytes 884760
  5.7 0.0 copy-start.2
  5.7 1.0 %copy-done.2 = bf16[8,4,16,384]{3,2,1,0:T(8,128)(2,1)S(1)} copy-done((bf16[8,4,16,384]{3,2,1,0:T(8,128)(2,1)S(1)}, bf16[8,4,16,384]{3,2,1,0:T(8,128)(2,1)}, u32[]{:S(2)}) %copy-start.2) | copy-done | bytes 393240
  6.6 0.0 copy-start.3
  6.6 0.7 %copy-done.3 = f32[192]{0:T(256)S(1)} copy-done((f32[192]{0:T(256)S(1)}, f32[192]{0:T(256)}, u32[]{:S(2)}) %copy-start.3) | copy-done | bytes 792
  7.3 0.0 copy-start.4
  7.3 0.7 %copy-done.4 = f32[192]{0:T(256)S(1)} copy-done((f32[192]{0:T(256)S(1)}, f32[192]{0:T(256)}, u32[]{:S(2)}) %copy-start.4) | copy-done | bytes 792
  8.0 0.0 copy-start.5
  8.0 0.7 %copy-done.5 = s32[16]{0:T(128)S(1)} copy-done((s32[16]{0:T(128)S(1)}, s32[16]{0:T(128)}, u32[]{:S(2)}) %copy-start.5) | copy-done | bytes 88
  8.7 21.9 %section.1 = bf16[4,2,8,384]{3,2,1,0:T(8,128)(2,1)S(1)} custom-call(bf16[8,4,16,384]{3,2,1,0:T(8,128)(2,1)S(1)} %copy-done.2, s32[16]{0:T(128)S(1)} %copy-done.5, bf16[9,384,384]{2,1,0:T(8,128)(2,1)S(1)} %copy-done, f32[1,384]{1,0:T(1,128)S(1)} %reshape.18.spatial_bias, bf16[3,384,384]{2,1,0:T(8,128)(2,1)S(1)} %copy-done.1, f32[1,384]{1,0:T(1,128)S(1)} %reshape.19.time_bias, ...), custom_call_target="tpu_custom_call" | custom-call | tf_op jit(solution)/shard_map/section/pallas_call | solution.py:345
  30.6 0.6 %copy.14 = bf16[4,2,8,384]{3,2,1,0:T(8,128)(2,1)} copy(bf16[4,2,8,384]{3,2,1,0:T(8,128)(2,1)S(1)} %section.1) | data formatting | bytes 98304
Async XLA Ops:
  2.7 1.7 %copy-start = (bf16[9,384,384]{2,1,0:T(8,128)(2,1)S(1)}, bf16[9,384,384]{2,1,0:T(8,128)(2,1)}, u32[]{:S(2)}) copy-start(bf16[9,384,384]{2,1,0:T(8,128)(2,1)} %down_weight.1) | copy-start | bytes 7962628
  4.5 1.2 %copy-start.1 = (bf16[3,384,384]{2,1,0:T(8,128)(2,1)S(1)}, bf16[3,384,384]{2,1,0:T(8,128)(2,1)}, u32[]{:S(2)}) copy-start(bf16[3,384,384]{2,1,0:T(8,128)(2,1)} %time_weight.1) | copy-start | bytes 2654212
  5.7 1.0 %copy-start.2 = (bf16[8,4,16,384]{3,2,1,0:T(8,128)(2,1)S(1)}, bf16[8,4,16,384]{3,2,1,0:T(8,128)(2,1)}, u32[]{:S(2)}) copy-start(bf16[8,4,16,384]{3,2,1,0:T(8,128)(2,1)} %video.1) | copy-start | bytes 1179652
  6.6 0.7 %copy-start.3 = (f32[192]{0:T(256)S(1)}, f32[192]{0:T(256)}, u32[]{:S(2)}) copy-start(f32[192]{0:T(256)} %param.20) | copy-start | bytes 2308
  7.3 0.7 %copy-start.4 = (f32[192]{0:T(256)S(1)}, f32[192]{0:T(256)}, u32[]{:S(2)}) copy-start(f32[192]{0:T(256)} %param.23) | copy-start | bytes 2308
  8.0 0.7 %copy-start.5 = (s32[16]{0:T(128)S(1)}, s32[16]{0:T(128)}, u32[]{:S(2)}) copy-start(s32[16]{0:T(128)} %counts.1) | copy-start | bytes 196

commit v2 on v1

--- a/solution.py
+++ b/solution.py
@@ -37,17 +37,17 @@
 def kernel(
     shards,
     video,
-    counts,
+    counts_hbm,
     down_weight,
-    spatial_bias,
+    spatial_bias_hbm,
     time_weight,
-    time_bias,
-    gain1,
+    time_bias_hbm,
+    gain1_hbm,
     weight1,
-    bias1,
-    gain2,
+    bias1_hbm,
+    gain2_hbm,
     weight2,
-    bias2,
+    bias2_hbm,
     out,
     vid_v,
     halo_v,
@@ -82,6 +82,14 @@
     recv_sem,
     before_sem,
     prior_sem,
+    counts,
+    spatial_bias,
+    time_bias,
+    gain1,
+    bias1,
+    gain2,
+    bias2,
+    small_sem,
 ):
     shard = lax.axis_index("frames")
     row = lax.axis_index("rows")
@@ -117,6 +125,22 @@
         for r in range(2):
             pl.semaphore_signal(barrier, inc=1, device_id=(shard - 1, r), device_id_type=MESH)
 
+    small_copies = [
+        pltpu.make_async_copy(source, target, small_sem.at[k])
+        for k, (source, target) in enumerate(
+            [
+                (counts_hbm, counts),
+                (spatial_bias_hbm, spatial_bias),
+                (time_bias_hbm, time_bias),
+                (gain1_hbm, gain1),
+                (bias1_hbm, bias1),
+                (gain2_hbm, gain2),
+                (bias2_hbm, bias2),
+            ]
+        )
+    ]
+    for copy in small_copies:
+        copy.start()
     time_copy = pltpu.make_async_copy(time_weight, time_v, in_sem.at[1])
     time_copy.start()
 
@@ -130,12 +154,6 @@
                 copies[tap].start()
         return copies
 
-    w1_copies = start_weight(weight1, w1_v, w1_sem)
-    w2_copies = start_weight(weight2, w2_v, w2_sem)
-
-    own_count = counts[shard]
-    live = jnp.where(shard == 0, 1, own_count // 2)
-
     pl.semaphore_wait(
         barrier, 1 + jnp.where(has_next, 2, 0) + jnp.where(has_prev, 2, 0)
     )
@@ -171,6 +189,10 @@
                 at = tc * chans + begin
                 xs[line, :, at : at + LANES] = part.reshape(slots * cols, LANES).astype(BF16)
 
+    for copy in small_copies:
+        copy.wait()
+    own_count = counts[shard]
+    live = jnp.where(shard == 0, 1, own_count // 2)
     vid_copy.wait()
     for line in range(in_rows):
         spread(line, vid_v[:, line])
@@ -189,7 +211,7 @@
         taps = down_v[3 * tr : 3 * tr + 3].reshape(3 * chans, chans)
         part = jnp.dot(lines, taps, preferred_element_type=F32)
         total = part if total is None else total + part
-    reduced = (total + spatial_bias[...]).astype(BF16)
+    reduced = (total + spatial_bias[...].reshape(1, -1)).astype(BF16)
     red_own[...] = reduced
     red_copy = remote(red_own, red_other, 1, (shard, other))
     red_copy.start()
@@ -224,6 +246,7 @@
             buffer[...] = jnp.zeros_like(buffer)
 
     next_start(before_copies)
+    w1_copies = start_weight(weight1, w1_v, w1_sem)
     before_waits = [
         remote(last_red, before_v.at[r], 2, (shard, other), before_sem.at[r]) for r in range(2)
     ]
@@ -243,7 +266,7 @@
             timeline[0] = before_v[...].astype(F32).reshape(all_rows, cols, chans)
         part = jnp.dot(tap_frames(kt), time_v[kt], preferred_element_type=F32)
         merged = part if merged is None else merged + part
-    merged = merged + time_bias[...]
+    merged = merged + time_bias[...].reshape(1, -1)
     first = jnp.where(shard == 0, timeline[1].reshape(plane, chans), merged[:plane])
     latent = round16(jnp.concatenate([first, merged[plane:]], axis=0))
     lat_v[...] = latent.reshape(lat_v.shape)
@@ -267,18 +290,19 @@
         lines = patches[kt : kt + out_slots].reshape(out_slots * plane, 9 * chans)
         return dot_t(lines, target[:, 9 * kt * chans : 9 * (kt + 1) * chans])
 
-    act_one = round16(rms_silu(latent, gain1[...]))
+    act_one = round16(rms_silu(latent, gain1[...].reshape(1, -1)))
     place(2, out_slots, act_one)
     recent = padded[pl.ds(live, 2), 1 : 1 + all_rows, LEFT : LEFT + cols, :]
     last_act[...] = recent.reshape(2 * plane, chans).astype(BF16)
     act_copy = remote(last_act, prior_act, 4, (shard + 1, row))
     next_start([act_copy])
+    w2_copies = start_weight(weight2, w2_v, w2_sem)
     acc = conv_part(2, w1_v, w1_copies)
     prev_wait([act_copy], prior_act)
     place(0, 2, prior_act[...].astype(F32))
     for kt in (1, 0):
         acc = acc + conv_part(kt, w1_v, w1_copies)
-    part_one = (acc + bias1[...]).astype(BF16)
+    part_one = (acc + bias1[...].reshape(1, -1)).astype(BF16)
     h_own[...] = part_one
     h_copy = remote(h_own, h_other, 5, (shard, other))
     h_copy.start()
@@ -294,14 +318,14 @@
 
     h_copy.wait_recv()
     hidden = join(row, part_one.astype(F32), h_other[...].astype(F32))
-    place(2, out_slots, rms_silu(hidden, gain2[...]))
+    place(2, out_slots, rms_silu(hidden, gain2[...].reshape(1, -1)))
     acc = conv_part(2, w2_v, w2_copies)
     prev_wait(prior_waits, h_prior)
     hidden = jnp.concatenate([h_prior[0].astype(F32), h_prior[1].astype(F32)], axis=-1)
-    place(0, 2, rms_silu(hidden, gain2[...]))
+    place(0, 2, rms_silu(hidden, gain2[...].reshape(1, -1)))
     for kt in (1, 0):
         acc = acc + conv_part(kt, w2_v, w2_copies)
-    part_two = round16(acc + bias2[...]).reshape(out_slots, plane, half)
+    part_two = round16(acc + bias2[...].reshape(1, -1)).reshape(out_slots, plane, half)
     hid[2 : 2 + out_slots] = part_two
     rows_of = own_rows * cols
 
@@ -338,15 +362,13 @@
     all_rows = 2 * own_rows
     half = w1.shape[1]
     plane = all_rows * cols
-    hbm = pl.BlockSpec(memory_space=pl.ANY)
-    vmem = pl.BlockSpec(memory_space=pltpu.VMEM)
-    smem = pl.BlockSpec(memory_space=pltpu.SMEM)
+    hbm = pl.BlockSpec(memory_space=pltpu.HBM)
     dma = pltpu.SemaphoreType.DMA
     return pl.pallas_call(
         functools.partial(kernel, shards),
         out_shape=jax.ShapeDtypeStruct((out_slots, own_rows, cols, chans), BF16),
-        in_specs=[hbm, smem, hbm, vmem, hbm, vmem, vmem, hbm, vmem, vmem, hbm, vmem],
-        out_specs=vmem,
+        in_specs=[hbm] * 12,
+        out_specs=pl.BlockSpec(memory_space=pltpu.VMEM),
         scratch_shapes=[
             pltpu.VMEM(video.shape, BF16),
             pltpu.VMEM((slots, in_cols, chans), BF16),
@@ -381,25 +403,20 @@
             dma((9,)),
             dma((2,)),
             dma((2,)),
+            pltpu.SMEM(counts.shape, counts.dtype),
+            pltpu.VMEM(sbias.shape, F32),
+            pltpu.VMEM(tbias.shape, F32),
+            pltpu.VMEM(gain1.shape, F32),
+            pltpu.VMEM(b1.shape, F32),
+            pltpu.VMEM(gain2.shape, F32),
+            pltpu.VMEM(b2.shape, F32),
+            dma((7,)),
         ],
         compiler_params=pltpu.CompilerParams(
-            collective_id=0, has_side_effects=True, vmem_limit_bytes=48 * 1024 * 1024
+            collective_id=0, has_side_effects=True, vmem_limit_bytes=62 * 1024 * 1024
         ),
         name="section",
-    )(
-        video,
-        counts,
-        down,
-        sbias.reshape(1, -1),
-        time,
-        tbias.reshape(1, -1),
-        gain1.reshape(1, -1),
-        w1,
-        b1.reshape(1, -1),
-        gain2.reshape(1, -1),
-        w2,
-        b2.reshape(1, -1),
-    )
+    )(video, counts, down, sbias, time, tbias, gain1, w1, b1, gain2, w2, b2)
 
 
 def solution(mesh):

time: 31.6 us -> 23.1 us (0.73)
  local copies, waits for them, and re-layouts: 9.28 us -> 1.42 us
  Pallas kernels: 21.9 us -> 21.5 us
    unnamed x13 -> x1, local copies, waits for them, and re-layouts: 6.55 us -> 1.42 us
    reshape x4 -> x0, local copies, waits for them, and re-layouts: 2.73 us -> none  [the longest x1 0.68 us: per_device(): tbias.reshape(1, -1)]
    pallas_call x1, Pallas kernels: 21.9 us -> 21.5 us  [per_device(): pl.pallas_call(functools.partial(kernel, shards), out_shape=jax.ShapeDtyp...]
where the time goes in v2:
time: 23.1 us; the launch traced here: 22.9 us
  Pallas kernels  21.5 us (93%)
  local copies, waits for them, and re-layouts  1.42 us (6%)
    pallas_call x1, Pallas kernels, per_device(): pl.pallas_call(functools.partial(kernel, shards), out_shape=jax.ShapeDtyp...  21.5 us
    unnamed x1, local copies, waits for them, and re-layouts  1.42 us

profile of v2, /device:TPU:25, one launch (start us, length us, event | category | flops | bytes accessed | tf_op | source)
XLA Modules:
  0.0 22.9 jit_solution(10679499846587428687)
XLA Ops:
  0.0 21.5 %section.1 = bf16[4,2,8,384]{3,2,1,0:T(8,128)(2,1)} custom-call(bf16[8,4,16,384]{3,2,1,0:T(8,128)(2,1)} %video.1, s32[16]{0:T(128)} %counts_hbm.1, bf16[9,384,384]{2,1,0:T(8,128)(2,1)} %down_weight.1, f32[384]{0:T(512)} %spatial_bias_hbm.1, bf16[3,384,384]{2,1,0:T(8,128)(2,1)} %time_weight.1, f32[384]{0:T(512)} %time_bias_hbm.1, f32[384]{0:T(512)} %gain1_hbm.1, ...), custom_call_target="tpu_custom_call" | custom-call | tf_op jit(solution)/shard_map/section/pallas_call | solution.py:367
  21.5 1.4 %copy.14 = bf16[4,2,8,384]{3,2,1,0:T(8,128)(2,1)} copy(bf16[4,2,8,384]{3,2,1,0:T(8,128)(2,1)} %section.1) | data formatting | bytes 98304

commit v3 on v2

--- a/solution.py
+++ b/solution.py
@@ -31,7 +31,8 @@
 
 
 def dot_t(values, weight):
-    return lax.dot_general(values, weight, (((1,), (1,)), ((), ())), preferred_element_type=F32)
+    turned = lax.dot_general(weight, values, (((1,), (1,)), ((), ())), preferred_element_type=F32)
+    return turned.T
 
 
 def kernel(
@@ -255,22 +256,6 @@
     to_timeline(red_other[...], own_rows * other)
     time_copy.wait()
 
-    def tap_frames(kt):
-        frames = [timeline[2 * t + kt].reshape(plane, chans) for t in range(out_slots)]
-        return jnp.concatenate(frames, axis=0).astype(BF16)
-
-    merged = None
-    for kt in (2, 1, 0):
-        if kt == 0:
-            prev_wait(before_waits, before_v)
-            timeline[0] = before_v[...].astype(F32).reshape(all_rows, cols, chans)
-        part = jnp.dot(tap_frames(kt), time_v[kt], preferred_element_type=F32)
-        merged = part if merged is None else merged + part
-    merged = merged + time_bias[...].reshape(1, -1)
-    first = jnp.where(shard == 0, timeline[1].reshape(plane, chans), merged[:plane])
-    latent = round16(jnp.concatenate([first, merged[plane:]], axis=0))
-    lat_v[...] = latent.reshape(lat_v.shape)
-
     def place(first_frame, frames, values):
         padded[first_frame : first_frame + frames, 1 : 1 + all_rows, LEFT : LEFT + cols, :] = values.reshape(
             frames, all_rows, cols, chans
@@ -284,24 +269,61 @@
                     window[:, ki : ki + all_rows].reshape(frames, plane, chans).astype(BF16)
                 )
 
-    def conv_part(kt, target, copies):
-        for tap in range(9 * kt, 9 * kt + 9):
-            copies[tap].wait()
-        lines = patches[kt : kt + out_slots].reshape(out_slots * plane, 9 * chans)
-        return dot_t(lines, target[:, 9 * kt * chans : 9 * (kt + 1) * chans])
-
-    act_one = round16(rms_silu(latent, gain1[...].reshape(1, -1)))
-    place(2, out_slots, act_one)
-    recent = padded[pl.ds(live, 2), 1 : 1 + all_rows, LEFT : LEFT + cols, :]
-    last_act[...] = recent.reshape(2 * plane, chans).astype(BF16)
-    act_copy = remote(last_act, prior_act, 4, (shard + 1, row))
-    next_start([act_copy])
+    def conv(target, copies, prior):
+        def part(kt, first_slot, end_slot):
+            frames = end_slot - first_slot
+            lines = patches[kt + first_slot : kt + end_slot].reshape(frames * plane, 9 * chans)
+            return dot_t(lines, target[:, 9 * kt * chans : 9 * (kt + 1) * chans])
+
+        def arrive(kt):
+            for tap in range(9 * kt, 9 * kt + 9):
+                copies[tap].wait()
+
+        arrive(2)
+        total = part(2, 0, out_slots)
+        arrive(1)
+        one = part(1, 1, out_slots)
+        arrive(0)
+        two = part(0, 2, out_slots)
+        prior()
+        one = jnp.concatenate([part(1, 0, 1), one], axis=0)
+        two = jnp.concatenate([part(0, 0, 2), two], axis=0)
+        return total + one + two
+
+    def time_part(kt, first_slot, end_slot):
+        frames = [timeline[2 * t + kt].reshape(plane, chans) for t in range(first_slot, end_slot)]
+        lines = jnp.concatenate(frames, axis=0).astype(BF16)
+        return jnp.dot(lines, time_v[kt], preferred_element_type=F32)
+
+    base = time_part(2, 0, out_slots) + time_part(1, 0, out_slots) + time_bias[...].reshape(1, -1)
+    later = round16(base[plane:] + time_part(0, 1, out_slots))
+    lat_v[1:] = later.reshape((out_slots - 1,) + lat_v.shape[1:])
+    place(3, out_slots - 1, round16(rms_silu(later, gain1[...].reshape(1, -1))))
+    whole = timeline[1].reshape(plane, chans)
+    padded[2, 1 : 1 + all_rows, LEFT : LEFT + cols, :] = round16(
+        rms_silu(whole, gain1[...].reshape(1, -1))
+    ).reshape(all_rows, cols, chans)
+    act_copies = [remote(last_act.at[k], prior_act.at[k], 4 + 5 * k, (shard + 1, row)) for k in range(2)]
+
+    def recent(k):
+        frame = padded[live + k, 1 : 1 + all_rows, LEFT : LEFT + cols, :]
+        last_act[k] = frame.reshape(plane, chans).astype(BF16)
+        next_start([act_copies[k]])
+
+    recent(1)
+    prev_wait(before_waits, before_v)
+    timeline[0] = before_v[...].astype(F32).reshape(all_rows, cols, chans)
+    first = round16(jnp.where(shard == 0, whole, base[:plane] + time_part(0, 0, 1)))
+    lat_v[0] = first.reshape(all_rows, cols, chans)
+    place(2, 1, round16(rms_silu(first, gain1[...].reshape(1, -1))))
+    recent(0)
     w2_copies = start_weight(weight2, w2_v, w2_sem)
-    acc = conv_part(2, w1_v, w1_copies)
-    prev_wait([act_copy], prior_act)
-    place(0, 2, prior_act[...].astype(F32))
-    for kt in (1, 0):
-        acc = acc + conv_part(kt, w1_v, w1_copies)
+
+    def prior_one():
+        prev_wait(act_copies, prior_act)
+        place(0, 2, prior_act[...].astype(F32))
+
+    acc = conv(w1_v, w1_copies, prior_one)
     part_one = (acc + bias1[...].reshape(1, -1)).astype(BF16)
     h_own[...] = part_one
     h_copy = remote(h_own, h_other, 5, (shard, other))
@@ -319,12 +341,13 @@
     h_copy.wait_recv()
     hidden = join(row, part_one.astype(F32), h_other[...].astype(F32))
     place(2, out_slots, rms_silu(hidden, gain2[...].reshape(1, -1)))
-    acc = conv_part(2, w2_v, w2_copies)
-    prev_wait(prior_waits, h_prior)
-    hidden = jnp.concatenate([h_prior[0].astype(F32), h_prior[1].astype(F32)], axis=-1)
-    place(0, 2, rms_silu(hidden, gain2[...].reshape(1, -1)))
-    for kt in (1, 0):
-        acc = acc + conv_part(kt, w2_v, w2_copies)
+
+    def prior_two():
+        prev_wait(prior_waits, h_prior)
+        hidden = jnp.concatenate([h_prior[0].astype(F32), h_prior[1].astype(F32)], axis=-1)
+        place(0, 2, rms_silu(hidden, gain2[...].reshape(1, -1)))
+
+    acc = conv(w2_v, w2_copies, prior_two)
     part_two = round16(acc + bias2[...].reshape(1, -1)).reshape(out_slots, plane, half)
     hid[2 : 2 + out_slots] = part_two
     rows_of = own_rows * cols
@@ -340,7 +363,7 @@
 
     @pl.when(has_next)
     def _():
-        for copy in before_copies + [act_copy] + prior_copies:
+        for copy in before_copies + act_copies + prior_copies:
             copy.wait_send()
 
     @pl.when(row == 1)
@@ -386,8 +409,8 @@
             pltpu.VMEM((out_slots, all_rows, cols, chans), F32),
             pltpu.VMEM((2 + out_slots, all_rows + 2, cols + 16, chans), F32),
             pltpu.VMEM((2 + out_slots, plane, 9 * chans), BF16),
-            pltpu.VMEM((2 * plane, chans), BF16),
-            pltpu.VMEM((2 * plane, chans), BF16),
+            pltpu.VMEM((2, plane, chans), BF16),
+            pltpu.VMEM((2, plane, chans), BF16),
             pltpu.VMEM((2 + out_slots, plane, half), F32),
             pltpu.VMEM((out_slots * plane, half), BF16),
             pltpu.VMEM((out_slots * plane, half), BF16),
@@ -399,8 +422,8 @@
             dma((3,)),
             dma((27,)),
             dma((27,)),
-            dma((9,)),
-            dma((9,)),
+            dma((10,)),
+            dma((10,)),
             dma((2,)),
             dma((2,)),
             pltpu.SMEM(counts.shape, counts.dtype),

time: 23.1 us -> 20.4 us (0.88)
  Pallas kernels: 21.5 us -> 18.8 us
    pallas_call x1, Pallas kernels: 21.5 us -> 18.8 us  [per_device(): pl.pallas_call(functools.partial(kernel, shards), out_shape=jax.ShapeDtyp...]
where the time goes in v3:
time: 20.4 us; the launch traced here: 20.3 us
  Pallas kernels  18.8 us (92%)
  local copies, waits for them, and re-layouts  1.42 us (7%)
    pallas_call x1, Pallas kernels, per_device(): pl.pallas_call(functools.partial(kernel, shards), out_shape=jax.ShapeDtyp...  18.8 us
    unnamed x1, local copies, waits for them, and re-layouts  1.42 us

profile of v3, /device:TPU:25, one launch (start us, length us, event | category | flops | bytes accessed | tf_op | source)
XLA Modules:
  0.0 20.3 jit_solution(3939692731217411651)
XLA Ops:
  0.0 18.8 %section.1 = bf16[4,2,8,384]{3,2,1,0:T(8,128)(2,1)} custom-call(bf16[8,4,16,384]{3,2,1,0:T(8,128)(2,1)} %video.1, s32[16]{0:T(128)} %counts_hbm.1, bf16[9,384,384]{2,1,0:T(8,128)(2,1)} %down_weight.1, f32[384]{0:T(512)} %spatial_bias_hbm.1, bf16[3,384,384]{2,1,0:T(8,128)(2,1)} %time_weight.1, f32[384]{0:T(512)} %time_bias_hbm.1, f32[384]{0:T(512)} %gain1_hbm.1, ...), custom_call_target="tpu_custom_call" | custom-call | tf_op jit(solution)/shard_map/section/pallas_call | solution.py:390
  18.9 1.4 %copy.14 = bf16[4,2,8,384]{3,2,1,0:T(8,128)(2,1)} copy(bf16[4,2,8,384]{3,2,1,0:T(8,128)(2,1)} %section.1) | data formatting | bytes 98304
